TPU v7x, 32 devices: a whole 2x2x4 slice. The times are simulated.
32 devices in a mesh: grp: 4 (over y, core), dev: 8 (over z, x).
Axes of the slice: x: 2, y: 2, z: 4, core: 2. Of those that a mesh axis runs over, the one named last changes fastest.
Arguments:
- voltage_real: bfloat16 [2048, 110592], P(('grp', 'dev')), may hold values from -6 to 6
- voltage_imaginary: bfloat16 [2048, 110592], P(('grp', 'dev')), may hold values from -6 to 6
- filter_taps: float32 [16, 4096], replicated, may hold values from -1.5 to 1.5
- weights_re: float32 [8, 2048, 512], P('dev'), may hold values from -0.0625 to 0.0625
- weights_im: float32 [8, 2048, 512], P('dev'), may hold values from -0.0625 to 0.0625
- owners: int32 [2], replicated, may hold values from 0 to 7
- antenna_map: int32 [2048], replicated, may hold values from 0 to 2047, each once
Outputs:
- beam_power: float32 [2, 4096, 512], P(None, ('grp', 'dev'))
Inputs may be any that keep to these rules, and one draw needn't show every extreme that they name: `owners`: the index along dev of the device whose calibration serves each step. A permutation: voltage slot j carries antenna antenna_map[j].
All inputs are finite; a program needn't handle non-finite values.
Results may differ from a plain program's by a relative error of at most 0.0022.
Values may be sent and summed in bfloat16 or wider, within the bound.
A program may use at most 256 MiB of HBM per device.

v0:
```python
import math

import jax
import jax.numpy as jnp
from jax import lax
from jax.sharding import PartitionSpec as P

FREQ_CHANNELS = 4096
TAPS = 16
SPECTRA_PER_STEP = 6
STEPS = 2


def spread(value, axis, source):
    kept = jnp.where(lax.axis_index(axis) == source, value, 0).astype(value.dtype)
    return lax.psum(kept, axis)


def angle_table(row_count, column_count, modulus):
    row_ids = lax.broadcasted_iota(jnp.int32, (row_count, column_count), 0)
    col_ids = lax.broadcasted_iota(jnp.int32, (row_count, column_count), 1)
    products = row_ids * col_ids % modulus
    angles = products.astype(jnp.float32) * (2.0 * math.pi / modulus)
    return (jnp.cos(angles), jnp.sin(angles))


def fourier_transform(frames_re, frames_im):
    antenna_count = frames_re.shape[0]
    spectra = frames_re.shape[1]
    channels = frames_re.shape[2]
    outer_len = 2 ** ((channels.bit_length() - 1) // 2)
    inner_len = channels // outer_len
    layout_re = frames_re.reshape(antenna_count, spectra, outer_len, inner_len)
    layout_im = frames_im.reshape(antenna_count, spectra, outer_len, inner_len)
    cos_outer, sin_outer = angle_table(outer_len, outer_len, outer_len)
    high = lax.Precision.HIGHEST
    first_re = jnp.einsum("atnb,nk->atkb", layout_re, cos_outer, precision=high) + jnp.einsum(
        "atnb,nk->atkb", layout_im, sin_outer, precision=high
    )
    first_im = jnp.einsum("atnb,nk->atkb", layout_im, cos_outer, precision=high) - jnp.einsum(
        "atnb,nk->atkb", layout_re, sin_outer, precision=high
    )
    cos_twist, sin_twist = angle_table(outer_len, inner_len, channels)
    twist_re = first_re * cos_twist + first_im * sin_twist
    twist_im = first_im * cos_twist - first_re * sin_twist
    cos_inner, sin_inner = angle_table(inner_len, inner_len, inner_len)
    norm_factor = channels ** (-0.5)
    final_re = (
        jnp.einsum("atkb,bm->mkta", twist_re, cos_inner, precision=high)
        + jnp.einsum("atkb,bm->mkta", twist_im, sin_inner, precision=high)
    ) * norm_factor
    final_im = (
        jnp.einsum("atkb,bm->mkta", twist_im, cos_inner, precision=high)
        - jnp.einsum("atkb,bm->mkta", twist_re, sin_inner, precision=high)
    ) * norm_factor
    joined = jnp.stack([final_re.astype(jnp.bfloat16), final_im.astype(jnp.bfloat16)], 3)
    return joined.reshape(channels, spectra, 2 * antenna_count)


def detect(antenna_rows, cal_rows, antenna_per_device):
    weight_re = cal_rows[0]
    weight_im = cal_rows[1]
    column_count = weight_re.shape[1]
    block_count = weight_re.shape[0] // antenna_per_device
    upper = jnp.concatenate([weight_re, weight_im], 1).reshape(
        block_count, antenna_per_device, 2 * column_count
    )
    lower = jnp.concatenate([-weight_im, weight_re], 1).reshape(
        block_count, antenna_per_device, 2 * column_count
    )
    mixing = jnp.stack([upper, lower], 1).reshape(2 * weight_re.shape[0], 2 * column_count)
    beam_terms = jnp.einsum("fta,ab->ftb", antenna_rows, mixing, preferred_element_type=jnp.float32)
    return jnp.mean(
        beam_terms[..., :column_count] ** 2 + beam_terms[..., column_count:] ** 2, axis=1
    )


def on_device(
    voltage_real, voltage_imaginary, filter_taps, weights_re, weights_im, owners, antenna_map
):
    antenna_per_device = voltage_real.shape[0]
    blocks_re = voltage_real.reshape(antenna_per_device, -1, FREQ_CHANNELS)
    blocks_im = voltage_imaginary.reshape(antenna_per_device, -1, FREQ_CHANNELS)
    own_weights = jnp.stack(
        [
            jnp.take(weights_re[0].astype(jnp.bfloat16), antenna_map, axis=0),
            jnp.take(weights_im[0].astype(jnp.bfloat16), antenna_map, axis=0),
        ]
    )
    outputs = []
    for window_step in range(STEPS):
        offset = window_step * SPECTRA_PER_STEP
        frames_re = jnp.zeros((antenna_per_device, SPECTRA_PER_STEP, FREQ_CHANNELS), jnp.float32)
        frames_im = jnp.zeros((antenna_per_device, SPECTRA_PER_STEP, FREQ_CHANNELS), jnp.float32)
        for tap_index in range(TAPS):
            lower = offset + tap_index
            frames_re = (
                frames_re
                + blocks_re[:, lower : lower + SPECTRA_PER_STEP, :].astype(jnp.float32)
                * filter_taps[tap_index]
            )
            frames_im = (
                frames_im
                + blocks_im[:, lower : lower + SPECTRA_PER_STEP, :].astype(jnp.float32)
                * filter_taps[tap_index]
            )
        spectrum_rows = fourier_transform(frames_re, frames_im)
        antenna_rows = lax.all_to_all(
            spectrum_rows, ("grp", "dev"), split_axis=0, concat_axis=2, tiled=True
        )
        leader = owners[window_step]
        received = spread(own_weights, "dev", leader)
        beam_power = detect(antenna_rows, received, antenna_per_device)
        outputs.append(beam_power)
    return jnp.stack(outputs)


def solution(mesh):
    return jax.shard_map(
        on_device,
        mesh=mesh,
        in_specs=(
            P(("grp", "dev"), None),
            P(("grp", "dev"), None),
            P(),
            P("dev", None, None),
            P("dev", None, None),
            P(),
            P(),
        ),
        out_specs=P(None, ("grp", "dev"), None),
        check_vma=False,
    )
```

profile of v0, /device:TPU:0, one launch (start us, length us, event | category | flops | bytes accessed | tf_op | source)
XLA Modules:
  0.0 1334.8 jit_solution(12481701310058124082)
XLA Ops:
  8.9 16.3 %reshape.131 = bf16[64,27,4096]{2,1,0:T(8,128)(2,1)} reshape(bf16[64,110592]{1,0:T(8,128)(2,1)} %param.9) | data formatting | bytes 28311552 | tf_op jit(solution)/shard_map/reshape | solution.py:82
  25.2 46.7 %fusion.40 = f32[64,6,4096]{2,1,0:T(8,128)} fusion(bf16[64,27,4096]{2,1,0:T(8,128)(2,1)} %reshape.131, f32[4096]{0:T(1024)S(1)} %bitcast.243, f32[4096]{0:T(1024)S(1)} %bitcast.247, f32[4096]{0:T(1024)S(1)} %bitcast.191, f32[4096]{0:T(1024)S(1)} %bitcast.195, f32[4096]{0:T(1024)S(1)} %bitcast.199, f32[4096]{0:T(1024)S(1)} %bitcast.203, ...), kind=kLoop, calls=%fused_computation.92 | loop fusion | flops 73924608 | bytes 56885248 | tf_op jit(solution)/shard_map/add | solution.py:98
  71.9 12.7 reshape.171
  84.5 18.5 %fusion.102 = f32[64,64,6,64]{3,0,2,1:T(8,128)} fusion(f32[64,6,64,64]{3,2,1,0:T(8,128)} %reshape.171), kind=kOutput, calls=%fused_computation.167 | convolution fusion | flops 1208016896 | bytes 12582912 | tf_op jit(solution)/shard_map/atnb,nk->atkb/dot_general | solution.py:37
  103.0 14.0 %fusion.88 = f32[64,64,6,64]{3,0,2,1:T(8,128)} fusion(f32[64,6,64,64]{3,2,1,0:T(8,128)S(1)} %copy-done), kind=kOutput, calls=%fused_computation.153 | convolution fusion | flops 1208016896 | bytes 12582912 | tf_op jit(solution)/shard_map/atnb,nk->atkb/dot_general | solution.py:40
  117.0 16.3 %reshape.133 = bf16[64,27,4096]{2,1,0:T(8,128)(2,1)} reshape(bf16[64,110592]{1,0:T(8,128)(2,1)} %param.10) | data formatting | bytes 28311552 | tf_op jit(solution)/shard_map/reshape | solution.py:83
  133.3 46.2 %fusion.65 = f32[64,6,4096]{2,1,0:T(8,128)} fusion(bf16[64,27,4096]{2,1,0:T(8,128)(2,1)} %reshape.133, f32[4096]{0:T(1024)S(1)} %bitcast.244, f32[4096]{0:T(1024)S(1)} %bitcast.248, f32[4096]{0:T(1024)S(1)} %bitcast.192, f32[4096]{0:T(1024)S(1)} %bitcast.196, f32[4096]{0:T(1024)S(1)} %bitcast.200, f32[4096]{0:T(1024)S(1)} %bitcast.204, ...), kind=kLoop, calls=%fused_computation.117 | loop fusion | flops 73924608 | bytes 56885248 | tf_op jit(solution)/shard_map/add | solution.py:103
  179.4 12.7 reshape.172
  192.1 18.4 %fusion.100 = f32[64,64,6,64]{3,0,2,1:T(8,128)} fusion(f32[64,6,64,64]{3,2,1,0:T(8,128)} %reshape.172), kind=kOutput, calls=%fused_computation.165 | convolution fusion | flops 1208016896 | bytes 12582912 | tf_op jit(solution)/shard_map/atnb,nk->atkb/dot_general | solution.py:40
  210.5 14.0 %fusion.90 = f32[64,64,6,64]{3,0,2,1:T(8,128)} fusion(f32[64,6,64,64]{3,2,1,0:T(8,128)S(1)} %copy-done.1), kind=kOutput, calls=%fused_computation.155 | convolution fusion | flops 1208016896 | bytes 12582912 | tf_op jit(solution)/shard_map/atnb,nk->atkb/dot_general | solution.py:37
  224.5 46.3 %fusion.50 = f32[64,6,4096]{2,1,0:T(8,128)} fusion(bf16[64,27,4096]{2,1,0:T(8,128)(2,1)} %reshape.133, f32[4096]{0:T(1024)S(1)} %bitcast.245, f32[4096]{0:T(1024)S(1)} %bitcast.249, f32[4096]{0:T(1024)S(1)} %bitcast.193, f32[4096]{0:T(1024)S(1)} %bitcast.197, f32[4096]{0:T(1024)S(1)} %bitcast.201, f32[4096]{0:T(1024)S(1)} %bitcast.205, ...), kind=kLoop, calls=%fused_computation.102 | loop fusion | flops 73924608 | bytes 56885248 | tf_op jit(solution)/shard_map/add | solution.py:103
  270.8 47.9 %fusion.25 = f32[64,6,4096]{2,1,0:T(8,128)} fusion(bf16[64,27,4096]{2,1,0:T(8,128)(2,1)} %reshape.131, f32[4096]{0:T(1024)S(1)} %bitcast.246, f32[4096]{0:T(1024)S(1)} %bitcast.250, f32[4096]{0:T(1024)S(1)} %bitcast.194, f32[4096]{0:T(1024)S(1)} %bitcast.198, f32[4096]{0:T(1024)S(1)} %bitcast.202, f32[4096]{0:T(1024)S(1)} %bitcast.206, ...), kind=kLoop, calls=%fused_computation.77 | loop fusion | flops 73924608 | bytes 56885248 | tf_op jit(solution)/shard_map/add | solution.py:98
  318.6 12.6 reshape.169
  331.2 18.3 %fusion.108 = f32[64,64,6,64]{3,0,2,1:T(8,128)} fusion(f32[64,6,64,64]{3,2,1,0:T(8,128)} %reshape.169), kind=kOutput, calls=%fused_computation.173 | convolution fusion | flops 1208016896 | bytes 12582912 | tf_op jit(solution)/shard_map/atnb,nk->atkb/dot_general | solution.py:37
  349.6 14.0 %fusion.94 = f32[64,64,6,64]{3,0,2,1:T(8,128)} fusion(f32[64,6,64,64]{3,2,1,0:T(8,128)S(1)} %copy-done.2), kind=kOutput, calls=%fused_computation.159 | convolution fusion | flops 1208016896 | bytes 12582912 | tf_op jit(solution)/shard_map/atnb,nk->atkb/dot_general | solution.py:40
  363.8 12.6 reshape.170
  376.4 17.1 %fusion.96 = f32[64,64,6,64]{3,0,2,1:T(8,128)} fusion(f32[64,6,64,64]{3,2,1,0:T(8,128)} %reshape.170), kind=kOutput, calls=%fused_computation.161 | convolution fusion | flops 1208016896 | bytes 12582912 | tf_op jit(solution)/shard_map/atnb,nk->atkb/dot_general | solution.py:37
  393.6 49.0 %multiply_add_fusion.1 = (f32[64,64,6,64]{3,0,2,1:T(8,128)}, f32[64,64,6,64]{3,0,2,1:T(8,128)}, f32[64,64,6,64]{3,0,2,1:T(8,128)}, f32[64,64,6,64]{3,0,2,1:T(8,128)}) fusion(f32[64,64]{1,0:T(8,128)S(1)} %copy.55, f32[64,64]{1,0:T(8,128)S(1)} %copy.52, f32[64,64,6,64]{3,0,2,1:T(8,128)} %fusion.94, f32[64,64,6,64]{3,0,2,1:T(8,128)} %fusion.108, ...), kind=kOutput, calls=%fused_computation.27 | convolution fusion | flops 1233182720 | bytes 75530240 | tf_op jit(solution)/shard_map/atnb,nk->atkb/dot_general | solution.py:40
  442.7 43.4 %fusion.10 = f32[64,64,6,64]{3,0,2,1:T(8,128)} fusion(f32[64,64,6,64]{3,0,2,1:T(8,128)} %get-tuple-element.9), kind=kOutput, calls=%fused_computation.14 | convolution fusion | flops 1208016896 | bytes 12582912 | tf_op jit(solution)/shard_map/atkb,bm->mkta/dot_general | solution.py:50
  486.1 38.6 %fusion.8 = f32[64,64,6,64]{3,0,2,1:T(8,128)} fusion(f32[64,64,6,64]{3,0,2,1:T(8,128)S(1)} %bitcast.176), kind=kOutput, calls=%fused_computation.12 | convolution fusion | flops 1208016896 | bytes 12582912 | tf_op jit(solution)/shard_map/atkb,bm->mkta/dot_general | solution.py:53
  524.8 40.1 %fusion.66 = bf16[64,64,6,1,64]{1,0,2,4,3:T(8,128)(2,1)} fusion(f32[64,64,6,64]{3,0,2,1:T(8,128)} %fusion.10, f32[64,64,6,64]{3,0,2,1:T(8,128)S(1)} %bitcast.178), kind=kOutput, calls=%fused_computation.120 | convolution fusion | flops 1212735488 | bytes 15728640 | tf_op jit(solution)/shard_map/atkb,bm->mkta/dot_general | solution.py:49
  564.9 40.4 %fusion.67 = bf16[64,64,6,1,64]{1,0,2,4,3:T(8,128)(2,1)} fusion(f32[64,64,6,64]{3,0,2,1:T(8,128)} %fusion.8, f32[64,64,6,64]{3,0,2,1:T(8,128)S(1)} %bitcast.178), kind=kOutput, calls=%fused_computation.121 | convolution fusion | flops 1212735488 | bytes 15728640 | tf_op jit(solution)/shard_map/atkb,bm->mkta/dot_general | solution.py:54
  616.6 18.9 %reshape.167 = bf16[4096,6,128]{0,1,2:T(8,128)(2,1)} reshape(bf16[64,64,6,2,64]{1,0,2,4,3:T(8,128)(2,1)} %pad_maximum_fusion) | data formatting | bytes 12582912 | tf_op jit(solution)/shard_map/reshape | solution.py:57
  635.5 12.8 copy.57
  687.1 41.8 %fusion.2 = f32[64,64,6,64]{3,0,2,1:T(8,128)} fusion(f32[64,64,6,64]{3,0,2,1:T(8,128)} %get-tuple-element.34), kind=kOutput, calls=%fused_computation.6 | convolution fusion | flops 1208016896 | bytes 12582912 | tf_op jit(solution)/shard_map/atkb,bm->mkta/dot_general | solution.py:50
  729.0 43.0 %fusion.68 = bf16[64,64,6,1,64]{1,0,2,4,3:T(8,128)(2,1)} fusion(f32[64,64,6,64]{3,0,2,1:T(8,128)} %fusion.2, f32[64,64,6,64]{3,0,2,1:T(8,128)} %get-tuple-element.35), kind=kOutput, calls=%fused_computation.122 | convolution fusion | flops 1212735488 | bytes 15728640 | tf_op jit(solution)/shard_map/atkb,bm->mkta/dot_general | solution.py:49
  772.0 38.8 %fusion = f32[64,64,6,64]{3,0,2,1:T(8,128)} fusion(f32[64,64,6,64]{3,0,2,1:T(8,128)S(1)} %bitcast.174), kind=kOutput, calls=%fused_computation.4 | convolution fusion | flops 1208016896 | bytes 12582912 | tf_op jit(solution)/shard_map/atkb,bm->mkta/dot_general | solution.py:53
  810.9 41.2 %fusion.69 = bf16[64,64,6,1,64]{1,0,2,4,3:T(8,128)(2,1)S(1)} fusion(f32[64,64,6,64]{3,0,2,1:T(8,128)} %fusion, f32[64,64,6,64]{3,0,2,1:T(8,128)} %get-tuple-element.35), kind=kOutput, calls=%fused_computation.123 | convolution fusion | flops 1212735488 | bytes 15728640 | tf_op jit(solution)/shard_map/atkb,bm->mkta/dot_general | solution.py:54
  858.7 19.0 %reshape.168 = bf16[4096,6,128]{0,1,2:T(8,128)(2,1)} reshape(bf16[64,64,6,2,64]{1,0,2,4,3:T(8,128)(2,1)} %pad_maximum_fusion.1) | data formatting | bytes 12582912 | tf_op jit(solution)/shard_map/reshape | solution.py:57
  877.7 12.8 copy.71
  890.5 64.3 %all-to-all-done = bf16[4096,6,128]{2,1,0:T(8,128)(2,1)} async-done(((bf16[4096,6,128]{2,1,0:T(8,128)(2,1)}), bf16[4096,6,128]{2,1,0:T(8,128)(2,1)}, u32[]{:S(2)}, u32[]{:S(2)}) %all-to-all-start) | async-done | bytes 6291488 | tf_op jit(solution)/shard_map/all_to_all | solution.py:108
  958.5 291.7 %all-reduce.3.cloned.1.call-done = (bf16[2,2048,512]{2,1,0:T(8,128)(2,1)}, bf16[2,2048,512]{2,1,0:T(8,128)(2,1)}) async-done(((bf16[2,2048,512]{2,1,0:T(8,128)(2,1)}, bf16[2,2048,512]{2,1,0:T(8,128)(2,1)}), (bf16[2,2048,512]{2,1,0:T(8,128)(2,1)}, bf16[2,2048,512]{2,1,0:T(8,128)(2,1)})) %all-reduce.3.cloned.1.call-update) | async-done | bytes 8388624 | tf_op jit(solution)/shard_map/psum | solution.py:16
  (70 shorter events, 139.3 us)
Async XLA Ops:
  84.5 18.5 %copy-start = (f32[64,6,64,64]{3,2,1,0:T(8,128)S(1)}, f32[64,6,64,64]{3,2,1,0:T(8,128)}, u32[]{:S(2)}) copy-start(f32[64,6,64,64]{3,2,1,0:T(8,128)} %reshape.171) | copy-start | bytes 18874372
  192.1 18.4 %copy-start.1 = (f32[64,6,64,64]{3,2,1,0:T(8,128)S(1)}, f32[64,6,64,64]{3,2,1,0:T(8,128)}, u32[]{:S(2)}) copy-start(f32[64,6,64,64]{3,2,1,0:T(8,128)} %reshape.172) | copy-start | bytes 18874372
  331.2 18.4 %copy-start.2 = (f32[64,6,64,64]{3,2,1,0:T(8,128)S(1)}, f32[64,6,64,64]{3,2,1,0:T(8,128)}, u32[]{:S(2)}) copy-start(f32[64,6,64,64]{3,2,1,0:T(8,128)} %reshape.169) | copy-start | bytes 18874372
  442.7 43.5 %slice-start.3 = ((s8[12582912]{0:T(1024)(128)(4,1)}), s8[4194304]{0:T(1024)(128)(4,1)S(1)}, s32[]{:S(2)}) async-start(s8[12582912]{0:T(1024)(128)(4,1)} %bitcast.175), calls=%async_computation.6 | async-start | bytes 8388608
  442.7 43.5 %slice-start.4 = ((s8[12582912]{0:T(1024)(128)(4,1)}), s8[4194304]{0:T(1024)(128)(4,1)S(1)}, s32[]{:S(2)}) async-start(s8[12582912]{0:T(1024)(128)(4,1)} %bitcast.175), calls=%async_computation.7 | async-start | bytes 8388608
  442.7 43.4 %slice-start.5 = ((s8[12582912]{0:T(1024)(128)(4,1)}), s8[4194304]{0:T(1024)(128)(4,1)S(1)}, s32[]{:S(2)}) async-start(s8[12582912]{0:T(1024)(128)(4,1)} %bitcast.175), calls=%async_computation.8 | async-start | bytes 8388608
  442.7 82.1 %slice-start.6 = ((s8[12582912]{0:T(1024)(128)(4,1)}), s8[4194304]{0:T(1024)(128)(4,1)S(1)}, s32[]{:S(2)}) async-start(s8[12582912]{0:T(1024)(128)(4,1)} %bitcast.177), calls=%async_computation.9 | async-start | bytes 8388608
  442.7 82.1 %slice-start.7 = ((s8[12582912]{0:T(1024)(128)(4,1)}), s8[4194304]{0:T(1024)(128)(4,1)S(1)}, s32[]{:S(2)}) async-start(s8[12582912]{0:T(1024)(128)(4,1)} %bitcast.177), calls=%async_computation.10 | async-start | bytes 8388608
  486.1 38.6 %slice-start.8 = ((s8[12582912]{0:T(1024)(128)(4,1)}), s8[4194304]{0:T(1024)(128)(4,1)S(1)}, s32[]{:S(2)}) async-start(s8[12582912]{0:T(1024)(128)(4,1)} %bitcast.177), calls=%async_computation.11 | async-start | bytes 8388608
  648.3 7.5 copy-start.4
  648.3 306.6 %all-to-all-start = ((bf16[4096,6,128]{2,1,0:T(8,128)(2,1)}), bf16[4096,6,128]{2,1,0:T(8,128)(2,1)}, u32[]{:S(2)}, u32[]{:S(2)}) async-start(bf16[4096,6,128]{2,1,0:T(8,128)(2,1)} %copy.57), calls=%async_computation | async-start | bytes 16777216 | tf_op jit(solution)/shard_map/all_to_all | solution.py:108
  655.7 594.5 %all-reduce.3.cloned.1.call-start = ((), (), s32[]{:S(2)}) async-start(), calls=%async_computation.2 | async-start | bytes 16777216 | tf_op jit(solution)/shard_map/psum | solution.py:16
  669.9 9.2 copy-start.5
  729.0 43.0 %slice-start = ((s8[12582912]{0:T(1024)(128)(4,1)}), s8[4194304]{0:T(1024)(128)(4,1)S(1)}, s32[]{:S(2)}) async-start(s8[12582912]{0:T(1024)(128)(4,1)} %bitcast.173), calls=%async_computation.3 | async-start | bytes 8388608
  729.0 43.0 %slice-start.1 = ((s8[12582912]{0:T(1024)(128)(4,1)}), s8[4194304]{0:T(1024)(128)(4,1)S(1)}, s32[]{:S(2)}) async-start(s8[12582912]{0:T(1024)(128)(4,1)} %bitcast.173), calls=%async_computation.4 | async-start | bytes 8388608
  729.0 43.0 %slice-start.2 = ((s8[12582912]{0:T(1024)(128)(4,1)}), s8[4194304]{0:T(1024)(128)(4,1)S(1)}, s32[]{:S(2)}) async-start(s8[12582912]{0:T(1024)(128)(4,1)} %bitcast.173), calls=%async_computation.5 | async-start | bytes 8388608
  810.9 41.2 %copy-start.3 = (bf16[64,64,6,1,64]{1,0,2,4,3:T(8,128)(2,1)S(1)}, bf16[64,64,6,1,64]{1,0,2,4,3:T(8,128)(2,1)}, u32[]{:S(2)}) copy-start(bf16[64,64,6,1,64]{1,0,2,4,3:T(8,128)(2,1)} %fusion.68) | copy-start | bytes 9437188
  954.8 340.1 %all-to-all-start.1 = ((bf16[4096,6,128]{2,1,0:T(8,128)(2,1)}), bf16[4096,6,128]{2,1,0:T(8,128)(2,1)}, u32[]{:S(2)}, u32[]{:S(2)}) async-start(bf16[4096,6,128]{2,1,0:T(8,128)(2,1)} %copy.71), calls=%async_computation.1 | async-start | bytes 16777216 | tf_op jit(solution)/shard_map/all_to_all | solution.py:108
Sparse Core Ops, SparseCore 0:
  687.2 562.9 all-reduce.2
where the time goes:
time: 1350 us; the launch traced here: 1330 us
  matrix products  513 us (38%)
  waiting for transfers between devices  356 us (26%)
  other arithmetic  227 us (17%)
  local copies, waits for them, and re-layouts  213 us (16%)
  between operations  15.3 us (1%)
    psum x1, waiting for transfers between devices, spread(): return lax.psum(kept, axis)  292 us
    add x2, other arithmetic, on_device(): frames_re + blocks_re[:, lower:lower + SPECTRA_PER_STEP, :].astype(jnp.fl...  94.5 us
    add x2, other arithmetic, on_device(): frames_im + blocks_im[:, lower:lower + SPECTRA_PER_STEP, :].astype(jnp.fl...  92.4 us
    dot_general x2, matrix products, fourier_transform(): jnp.einsum('atkb,bm->mkta', twist_im, sin_inner, precision=high)  85.2 us
    dot_general x2, matrix products, fourier_transform(): jnp.einsum('atkb,bm->mkta', twist_re, cos_inner, precision=high)  83.1 us
    dot_general x2, matrix products, fourier_transform(): jnp.einsum('atkb,bm->mkta', twist_re, sin_inner, precision=high)  81.6 us
    dot_general x2, matrix products, fourier_transform(): jnp.einsum('atkb,bm->mkta', twist_im, cos_inner, precision=high)  77.5 us
    dot_general x2, matrix products, fourier_transform(): jnp.einsum('atnb,nk->atkb', layout_im, cos_outer, precision=high)  67.4 us
  transfers between devices with their start and end apart: 3, of which 2 were waited for; matrix products, arithmetic and copies ran while one was open for 20% of the time, Pallas kernels for 0%

commit v1 on v0

v1 whole, which is shorter than its diff:
```python
import functools
import math

import jax
import jax.numpy as jnp
import ml_dtypes
import numpy as np
from jax import lax
from jax.experimental import pallas as pl
from jax.experimental.pallas import tpu as pltpu
from jax.sharding import PartitionSpec as P

FREQ_CHANNELS = 4096
TAPS = 16
SPECTRA_PER_STEP = 6
STEPS = 2
LANES = 128
OUTER = FREQ_CHANNELS // LANES
ANT_BLOCK = 16


def dft_tables():
    f1 = np.arange(OUTER)[:, None, None]
    f2 = np.arange(LANES)[None, :, None]
    n2 = np.arange(LANES)[None, None, :]
    angle = (n2 * (f1 + OUTER * f2) % FREQ_CHANNELS) * (2.0 * math.pi / FREQ_CHANNELS)
    c = np.cos(angle) / math.sqrt(FREQ_CHANNELS)
    s = np.sin(angle) / math.sqrt(FREQ_CHANNELS)
    real = np.concatenate([c, s], -1).reshape(OUTER, OUTER, 4, 2 * LANES)
    imag = np.concatenate([-s, c], -1).reshape(OUTER, OUTER, 4, 2 * LANES)
    odd = (np.arange(OUTER) % 2 == 1)[:, None, None, None]
    first = np.where(odd, imag, real)
    second = np.where(odd, real, imag)
    table = np.stack([first, second], 2).reshape(OUTER, 2 * LANES, 2 * LANES)
    high = table.astype(ml_dtypes.bfloat16)
    low = (table - high.astype(np.float64)).astype(ml_dtypes.bfloat16)
    return high, low


def rotate(value, k, length):
    re, im = value
    k = k % length
    if k == 0:
        return re, im
    if 4 * k == length:
        return im, -re
    if 2 * k == length:
        return -re, -im
    if 4 * k == 3 * length:
        return -im, re
    c, s = math.cos(2 * math.pi * k / length), math.sin(2 * math.pi * k / length)
    if 8 * k == length:
        return (re + im) * c, (im - re) * c
    if 8 * k == 3 * length:
        return (im - re) * s, (re + im) * (-s)
    return re * c + im * s, im * c - re * s


def small_fft(values):
    count = len(values)
    if count == 1:
        return values
    even = small_fft(values[0::2])
    odd = small_fft(values[1::2])
    low, high = [], []
    for k in range(count // 2):
        a = even[k]
        b = rotate(odd[k], k, count)
        low.append((a[0] + b[0], a[1] + b[1]))
        high.append((a[0] - b[0], a[1] - b[1]))
    return low + high


def channelize_kernel(step, ants, vr_ref, vi_ref, taps_ref, wh_ref, wl_ref, out_ref, fr_ref, fi_ref, xs_ref):
    block = pl.program_id(0)
    offset = step * SPECTRA_PER_STEP

    @pl.loop(0, OUTER)
    def _(n1):
        lane = pl.multiple_of(n1 * LANES, LANES)
        taps = [jnp.broadcast_to(taps_ref[k : k + 1, pl.ds(lane, LANES)], (8, LANES)) for k in range(TAPS)]
        for v_ref, f_ref in ((vr_ref, fr_ref), (vi_ref, fi_ref)):
            acc = [[None, None] for _ in range(SPECTRA_PER_STEP)]
            for b in range(SPECTRA_PER_STEP + TAPS - 1):
                start = pl.multiple_of((offset + b) * FREQ_CHANNELS + lane, LANES)
                value = v_ref[:, pl.ds(start, LANES)].astype(jnp.float32)
                for h in range(2):
                    half = value[8 * h : 8 * h + 8]
                    for t in range(SPECTRA_PER_STEP):
                        k = b - t
                        if 0 <= k < TAPS:
                            term = half * taps[k]
                            acc[t][h] = term if acc[t][h] is None else acc[t][h] + term
            for t in range(SPECTRA_PER_STEP):
                for h in range(2):
                    f_ref[t, h, n1] = acc[t][h]

    @pl.loop(0, SPECTRA_PER_STEP)
    def _(t):
        for h in range(2):
            values = [(fr_ref[t, h, n1], fi_ref[t, h, n1]) for n1 in range(OUTER)]
            result = small_fft(values)
            row = pl.multiple_of(t * ants + block * ANT_BLOCK + 8 * h, 8)
            for f1 in range(OUTER):
                xs_ref[f1, pl.ds(row, 8), 0:LANES] = result[f1][0]
                xs_ref[f1, pl.ds(row, 8), LANES : 2 * LANES] = result[f1][1]

    @pl.when(block == pl.num_programs(0) - 1)
    def _():
        columns = SPECTRA_PER_STEP * ants
        nt = functools.partial(
            lax.dot_general,
            dimension_numbers=(((1,), (1,)), ((), ())),
            preferred_element_type=jnp.float32,
        )

        @pl.loop(0, OUTER // 2)
        def _(pair):
            parts = []
            for lo in range(2):
                f1 = 2 * pair + lo
                x = xs_ref[f1]
                xh = x.astype(jnp.bfloat16)
                xl = (x - xh.astype(jnp.float32)).astype(jnp.bfloat16)
                wh = wh_ref[f1]
                y = nt(wh, xh) + nt(wl_ref[f1], xh) + nt(wh, xl)
                parts.append(y.reshape(OUTER, 8, columns))
            a, b = parts
            top = lax.broadcasted_iota(jnp.int32, (OUTER, 8, columns), 1) < 4
            re = jnp.where(top, a, b)
            im = pltpu.roll(jnp.where(top, b, a), 4, 1)
            out_ref[:, pair] = jnp.concatenate([re, im], 1).astype(jnp.bfloat16)


def channelize(step, voltage_real, voltage_imaginary, filter_taps, high, low):
    ants, samples = voltage_real.shape
    columns = SPECTRA_PER_STEP * ants
    once = pl.Buffered(1)
    stream = pl.BlockSpec((ANT_BLOCK, samples), lambda i: (i, 0))
    table = pl.BlockSpec((OUTER, 2 * LANES, 2 * LANES), lambda i: (0, 0, 0), pipeline_mode=once)
    return pl.pallas_call(
        functools.partial(channelize_kernel, step, ants),
        grid=(ants // ANT_BLOCK,),
        in_specs=[
            stream,
            stream,
            pl.BlockSpec((TAPS, FREQ_CHANNELS), lambda i: (0, 0), pipeline_mode=once),
            table,
            table,
        ],
        out_specs=pl.BlockSpec((OUTER, 16, 16, columns), lambda i: (0, 0, 0, 0), pipeline_mode=once),
        out_shape=jax.ShapeDtypeStruct((OUTER, 16, 16, columns), jnp.bfloat16),
        scratch_shapes=[
            pltpu.VMEM((SPECTRA_PER_STEP, 2, OUTER, 8, LANES), jnp.float32),
            pltpu.VMEM((SPECTRA_PER_STEP, 2, OUTER, 8, LANES), jnp.float32),
            pltpu.VMEM((OUTER, columns, 2 * LANES), jnp.float32),
        ],
        compiler_params=pltpu.CompilerParams(vmem_limit_bytes=56 * 2**20),
        cost_estimate=pl.CostEstimate(
            flops=20_000_000_000, bytes_accessed=50_000_000, transcendentals=0
        ),
        name="channelize",
    )(voltage_real, voltage_imaginary, filter_taps, high, low)


def detect_kernel(sources, ants, x_ref, w_ref, out_ref, xs_ref):
    rows = x_ref.shape[1]
    for t in range(SPECTRA_PER_STEP):
        for pair in range(sources // 2):
            xs_ref[t * rows : (t + 1) * rows, 2 * pair * ants : 2 * (pair + 1) * ants] = jnp.concatenate(
                [x_ref[2 * pair + j, :, t * ants : (t + 1) * ants] for j in range(2)], 1
            )
    beams = w_ref.shape[1] // 2
    total = None
    for t in range(SPECTRA_PER_STEP):
        g = jnp.dot(xs_ref[t * rows : (t + 1) * rows], w_ref[...], preferred_element_type=jnp.float32)
        g = g.reshape(rows // 16, 2, 8, 2 * beams)
        re, im = g[:, 0], g[:, 1]
        beam_re = re[..., :beams] - im[..., beams:]
        beam_im = re[..., beams:] + im[..., :beams]
        power = beam_re * beam_re + beam_im * beam_im
        total = power if total is None else total + power
    out_ref[...] = (total * (1.0 / SPECTRA_PER_STEP)).reshape(rows // 2, beams)


def detect(received, weights, sources):
    rows, columns = received.shape[1], received.shape[2]
    ants = columns // SPECTRA_PER_STEP
    beams = weights.shape[1] // 2
    block = rows // 2
    power = pl.pallas_call(
        functools.partial(detect_kernel, sources, ants),
        grid=(2,),
        in_specs=[
            pl.BlockSpec((sources, block, columns), lambda i: (0, i, 0)),
            pl.BlockSpec(weights.shape, lambda i: (0, 0), pipeline_mode=pl.Buffered(1)),
        ],
        out_specs=pl.BlockSpec((block // 2, beams), lambda i: (i, 0)),
        out_shape=jax.ShapeDtypeStruct((rows // 2, beams), jnp.float32),
        scratch_shapes=[pltpu.VMEM((SPECTRA_PER_STEP * block, sources * ants), jnp.bfloat16)],
        compiler_params=pltpu.CompilerParams(vmem_limit_bytes=48 * 2**20),
        cost_estimate=pl.CostEstimate(flops=6_500_000_000, bytes_accessed=11_000_000, transcendentals=0),
        name="detect",
    )(received, weights)
    return power.reshape(OUTER, 4, beams).swapaxes(0, 1).reshape(rows // 2, beams)


def detect_any(received, weights, sources, owned):
    ants = received.shape[-1]
    beams = weights.shape[1] // 2
    rows = received.transpose(4, 1, 3, 5, 2, 0, 6).reshape(
        OUTER * owned, SPECTRA_PER_STEP, 2, sources * ants
    )
    terms = jnp.einsum("ftpa,ab->ftpb", rows, weights, preferred_element_type=jnp.float32)
    beam_re = terms[:, :, 0, :beams] - terms[:, :, 1, beams:]
    beam_im = terms[:, :, 0, beams:] + terms[:, :, 1, :beams]
    return jnp.mean(beam_re**2 + beam_im**2, axis=1)


def on_device(groups, members, vr, vi, filter_taps, weights_re, weights_im, owners, antenna_map):
    devices = groups * members
    ants = vr.shape[0]
    total_ants = antenna_map.shape[0]
    quarter = total_ants // groups
    rows = lax.dynamic_slice_in_dim(antenna_map, lax.axis_index("grp") * quarter, quarter)
    own = jnp.concatenate(
        [
            jnp.take(weights_re[0], rows, axis=0).astype(jnp.bfloat16),
            jnp.take(weights_im[0], rows, axis=0).astype(jnp.bfloat16),
        ],
        1,
    )
    mine = lax.axis_index("dev") == owners
    kept = jnp.where(mine[:, None, None], own[None], 0).astype(jnp.bfloat16)
    weights = lax.all_gather(lax.psum(kept, "dev"), "grp", axis=1, tiled=True)

    high, low = (jnp.asarray(table) for table in dft_tables())
    owned = LANES // devices
    sent = []
    for step in range(STEPS):
        spectra = channelize(step, vr, vi, filter_taps, high, low)
        if devices != OUTER:
            spectra = spectra.reshape(OUTER, 16, 2, 2, 4 // owned, owned, SPECTRA_PER_STEP * ants)
            spectra = spectra.transpose(0, 4, 1, 2, 3, 5, 6)
        spectra = spectra.reshape(devices, -1, SPECTRA_PER_STEP * ants)
        sent.append(lax.all_to_all(spectra, ("grp", "dev"), split_axis=0, concat_axis=0, tiled=True))
    outputs = []
    for step in range(STEPS):
        if devices == OUTER:
            outputs.append(detect(sent[step], weights[step], devices))
        else:
            received = sent[step].reshape(devices, 16, 2, 2, owned, SPECTRA_PER_STEP, ants)
            outputs.append(detect_any(received, weights[step], devices, owned))
    return jnp.stack(outputs)


def solution(mesh):
    groups, members = mesh.shape["grp"], mesh.shape["dev"]
    return jax.shard_map(
        functools.partial(on_device, groups, members),
        mesh=mesh,
        in_specs=(
            P(("grp", "dev"), None),
            P(("grp", "dev"), None),
            P(),
            P("dev", None, None),
            P("dev", None, None),
            P(),
            P(),
        ),
        out_specs=P(None, ("grp", "dev"), None),
        check_vma=False,
    )
```

time: 1350 us -> 450 us (0.33); the launches traced: 1330 us -> 449 us
  matrix products: 513 us -> 0 us
  other arithmetic: 227 us -> 3.51 us
  local copies, waits for them, and re-layouts: 213 us -> 16.2 us
  Pallas kernels: 0 us -> 92.7 us
  waiting for transfers between devices: 356 us -> 312 us
    dot_general x18 -> x0, matrix products: 513 us -> none  [the longest x2 85.2 us: fourier_transform(): jnp.einsum('atkb,bm->mkta', twist_im, sin_inner, precision=high)]
    add x4 -> x0, other arithmetic: 187 us -> none  [the longest x2 94.5 us: on_device(): frames_re + blocks_re[:, lower:lower + SPECTRA_PER_STEP, :].astype(jnp.fl...]
    reshape x10 -> x2, local copies, waits for them, and re-layouts: 147 us -> 0.15 us  [detect(): power.reshape(OUTER, 4, beams).swapaxes(0, 1).reshape(rows // 2, beams)]
    psum x1, waiting for transfers between devices: 292 us -> 186 us  [on_device(): weights = lax.all_gather(lax.psum(kept, 'dev'), 'grp', axis=1, tiled=True)]
    pallas_call x0 -> x4, Pallas kernels: none -> 92.7 us  [the longest x2 74.8 us: channelize(): pl.pallas_call(functools.partial(channelize_kernel, step, ants), grid=(an...]
    all_gather x0 -> x1, waiting for transfers between devices: none -> 71.6 us  [on_device(): weights = lax.all_gather(lax.psum(kept, 'dev'), 'grp', axis=1, tiled=True)]
    all_to_all x4 -> x0, local copies, waits for them, and re-layouts: 40.9 us -> none  [on_device(): lax.all_to_all(spectrum_rows, ('grp', 'dev'), split_axis=0, concat_axis=2...]
    another operation x5 -> x0, other arithmetic: 28.2 us -> none  [the longest x2 17.9 us: fourier_transform(): jnp.stack([final_re.astype(jnp.bfloat16), final_im.astype(jnp.bfloat16)], 3)]
  transfers between devices with their start and end apart: 3 -> 4, of which waited for: 2 -> 3; matrix products, arithmetic and copies ran while one was open for 20% -> 4% of each run, Pallas kernels for 0% -> 10%
where the time goes in v1:
time: 450 us; the launch traced here: 449 us
  waiting for transfers between devices  312 us (69%)
  Pallas kernels  92.7 us (21%)
  local copies, waits for them, and re-layouts  16.2 us (4%)
  between operations  13.5 us (3%)
  starting transfers between devices  11.3 us (3%)
    psum x1, waiting for transfers between devices, on_device(): weights = lax.all_gather(lax.psum(kept, 'dev'), 'grp', axis=1, tiled=True)  186 us
    pallas_call x2, Pallas kernels, channelize(): pl.pallas_call(functools.partial(channelize_kernel, step, ants), grid=(an...  74.8 us
    all_gather x1, waiting for transfers between devices, on_device(): weights = lax.all_gather(lax.psum(kept, 'dev'), 'grp', axis=1, tiled=True)  71.6 us
    all_to_all x2, waiting for transfers between devices, on_device(): lax.all_to_all(spectra, ('grp', 'dev'), split_axis=0, concat_axis=0, tile...  54 us
    pallas_call x2, Pallas kernels, detect(): pl.pallas_call(functools.partial(detect_kernel, sources, ants), grid=(2,)...  17.9 us
    all_to_all x2, starting transfers between devices, on_device(): lax.all_to_all(spectra, ('grp', 'dev'), split_axis=0, concat_axis=0, tile...  11.2 us
  transfers between devices with their start and end apart: 4, of which 3 were waited for; matrix products, arithmetic and copies ran while one was open for 4% of the time, Pallas kernels for 10%

profile of v1, /device:TPU:0, one launch (start us, length us, event | category | flops | bytes accessed | tf_op | source)
XLA Modules:
  0.0 449.2 jit_solution(4874850005177134578)
XLA Ops:
  6.5 37.3 %channelize.3 = bf16[32,16,16,384]{3,2,1,0:T(8,128)(2,1)} custom-call(bf16[64,110592]{1,0:T(8,128)(2,1)} %vr_ref.3, bf16[64,110592]{1,0:T(8,128)(2,1)} %vi_ref.3, f32[16,4096]{1,0:T(8,128)} %taps_ref.3, bf16[32,256,256]{2,1,0:T(8,128)(2,1)} %constant.30.clone.wh_ref, bf16[32,256,256]{2,1,0:T(8,128)(2,1)} %constant.31.clone.wl_ref), custom_call_target="tpu_custom_call" | custom-call | flops 20000000000 | bytes 50000000 | tf_op jit(solution)/shard_map/channelize/pallas_call | solution.py:141
  43.8 7.4 %all-to-all-start.1 = ((bf16[32,256,384]{2,1,0:T(8,128)(2,1)}), bf16[32,256,384]{2,1,0:T(8,128)(2,1)}, u32[]{:S(2)}, u32[]{:S(2)}) async-start(bf16[32,256,384]{2,1,0:T(8,128)(2,1)} %bitcast.12), calls=%async_computation.1 | async-start | bytes 12582912 | tf_op jit(solution)/shard_map/all_to_all | solution.py:246
  51.2 0.0 all-reduce.2.cloned.1.call-start
  51.3 0.8 compare_and_fusion
  52.0 4.2 gather_fusion.1
  56.2 0.0 copy-start.1
  56.2 4.2 gather_fusion
  60.4 0.2 select_convert_fusion.1
  60.7 0.1 pad_maximum_fusion
  60.8 0.0 copy-done.1
  60.8 1.5 broadcast_select_fusion
  62.3 0.0 all-reduce.2.cloned.1.call-update
  62.4 0.0 all-gather.2.cloned.1.call-start
  62.4 186.4 %all-reduce.2.cloned.1.call-done = bf16[2,512,1024]{2,1,0:T(8,128)(2,1)} async-done(((bf16[2,512,1024]{2,1,0:T(8,128)(2,1)}), bf16[2,512,1024]{2,1,0:T(8,128)(2,1)}) %all-reduce.2.cloned.1.call-update) | async-done | bytes 2097168 | tf_op jit(solution)/shard_map/psum | solution.py:235
  248.8 0.0 all-gather.2.cloned.1.call-update
  248.9 37.5 %channelize.2 = bf16[32,16,16,384]{3,2,1,0:T(8,128)(2,1)} custom-call(bf16[64,110592]{1,0:T(8,128)(2,1)} %vr_ref.3, bf16[64,110592]{1,0:T(8,128)(2,1)} %vi_ref.3, f32[16,4096]{1,0:T(8,128)} %taps_ref.3, bf16[32,256,256]{2,1,0:T(8,128)(2,1)} %constant.30.clone.wh_ref, bf16[32,256,256]{2,1,0:T(8,128)(2,1)} %constant.31.clone.wl_ref), custom_call_target="tpu_custom_call" | custom-call | flops 20000000000 | bytes 50000000 | tf_op jit(solution)/shard_map/channelize/pallas_call | solution.py:141
  286.4 0.0 all-to-all-done.1.x_ref
  286.4 3.8 all-to-all-start
  290.2 71.6 %all-gather.2.cloned.1.call-done = bf16[2,2048,1024]{2,1,0:T(8,128)(2,1)} async-done(((bf16[2,512,1024]{2,1,0:T(8,128)(2,1)}), bf16[2,2048,1024]{2,1,0:T(8,128)(2,1)}) %all-gather.2.cloned.1.call-update) | async-done | bytes 8388624 | tf_op jit(solution)/shard_map/all_gather | solution.py:235
  361.8 5.3 %slice_bitcast_fusion.1 = (bf16[2048,1024]{1,0:T(8,128)(2,1)}, bf16[2048,1024]{1,0:T(8,128)(2,1)S(1)}) fusion(bf16[2,2048,1024]{2,1,0:T(8,128)(2,1)} %all-gather.2.cloned.1.call-done), kind=kLoop, calls=%fused_computation.3 | loop fusion | bytes 16777216 | tf_op jit(solution)/shard_map/squeeze | solution.py:250
  367.1 9.0 %detect.3 = f32[128,512]{1,0:T(8,128)S(1)} custom-call(bf16[32,256,384]{2,1,0:T(8,128)(2,1)} %all-to-all-done.1.x_ref, bf16[2048,1024]{1,0:T(8,128)(2,1)S(1)} %get-tuple-element.9.w_ref), custom_call_target="tpu_custom_call" | custom-call | flops 6499999744 | bytes 11000000 | tf_op jit(solution)/shard_map/detect/pallas_call | solution.py:191
  376.1 0.1 reshape.22
  376.2 0.1 copy.11
  376.3 54.0 %all-to-all-done.x_ref = bf16[32,256,384]{2,1,0:T(8,128)(2,1)} async-done(((bf16[32,256,384]{2,1,0:T(8,128)(2,1)}), bf16[32,256,384]{2,1,0:T(8,128)(2,1)}, u32[]{:S(2)}, u32[]{:S(2)}) %all-to-all-start) | async-done | bytes 6291488 | tf_op jit(solution)/shard_map/all_to_all | solution.py:246
  430.2 0.0 copy-start
  430.2 2.2 copy-done
  432.4 9.0 %detect.2 = f32[128,512]{1,0:T(8,128)S(1)} custom-call(bf16[32,256,384]{2,1,0:T(8,128)(2,1)} %all-to-all-done.x_ref, bf16[2048,1024]{1,0:T(8,128)(2,1)S(1)} %copy-done), custom_call_target="tpu_custom_call" | custom-call | flops 6499999744 | bytes 11000000 | tf_op jit(solution)/shard_map/detect/pallas_call | solution.py:191
  441.4 0.1 reshape.20
  441.5 0.1 copy.10
  441.6 0.8 pad_maximum_fusion.1
  (2 shorter events, 0.0 us)
Async XLA Ops:
  43.8 242.6 %all-to-all-start.1 = ((bf16[32,256,384]{2,1,0:T(8,128)(2,1)}), bf16[32,256,384]{2,1,0:T(8,128)(2,1)}, u32[]{:S(2)}, u32[]{:S(2)}) async-start(bf16[32,256,384]{2,1,0:T(8,128)(2,1)} %bitcast.12), calls=%async_computation.1 | async-start | bytes 12582912 | tf_op jit(solution)/shard_map/all_to_all | solution.py:246
  51.2 197.6 %all-reduce.2.cloned.1.call-start = ((), (), s32[]{:S(2)}) async-start(), calls=%async_computation.2 | async-start | bytes 4194304 | tf_op jit(solution)/shard_map/psum | solution.py:235
  56.2 4.6 %copy-start.1 = (s32[2]{0:T(128)S(1)}, s32[2]{0:T(128)}, u32[]{:S(2)}) copy-start(s32[2]{0:T(128)} %param.16) | copy-start | bytes 28
  62.4 299.5 %all-gather.2.cloned.1.call-start = ((), (), s32[]{:S(2)}) async-start(), calls=%async_computation.3 | async-start | bytes 10485760 | tf_op jit(solution)/shard_map/all_gather | solution.py:235
  286.4 143.9 %all-to-all-start = ((bf16[32,256,384]{2,1,0:T(8,128)(2,1)}), bf16[32,256,384]{2,1,0:T(8,128)(2,1)}, u32[]{:S(2)}, u32[]{:S(2)}) async-start(bf16[32,256,384]{2,1,0:T(8,128)(2,1)} %bitcast.13), calls=%async_computation | async-start | bytes 12582912 | tf_op jit(solution)/shard_map/all_to_all | solution.py:246
  430.2 2.2 copy-start
Sparse Core Ops, SparseCore 0:
  62.5 186.3 all-reduce.1
  250.4 111.3 all-gather.1

commit v2 on v1

--- a/solution.py
+++ b/solution.py
@@ -232,7 +232,8 @@
     )
     mine = lax.axis_index("dev") == owners
     kept = jnp.where(mine[:, None, None], own[None], 0).astype(jnp.bfloat16)
-    weights = lax.all_gather(lax.psum(kept, "dev"), "grp", axis=1, tiled=True)
+    kept, filter_taps = lax.optimization_barrier((kept, filter_taps))
+    summed = lax.psum(kept, "dev")
 
     high, low = (jnp.asarray(table) for table in dft_tables())
     owned = LANES // devices
@@ -243,7 +244,10 @@
             spectra = spectra.reshape(OUTER, 16, 2, 2, 4 // owned, owned, SPECTRA_PER_STEP * ants)
             spectra = spectra.transpose(0, 4, 1, 2, 3, 5, 6)
         spectra = spectra.reshape(devices, -1, SPECTRA_PER_STEP * ants)
+        if step == STEPS - 1:
+            spectra, summed = lax.optimization_barrier((spectra, summed))
         sent.append(lax.all_to_all(spectra, ("grp", "dev"), split_axis=0, concat_axis=0, tiled=True))
+    weights = lax.all_gather(summed, "grp", axis=1, tiled=True)
     outputs = []
     for step in range(STEPS):
         if devices == OUTER:

time: 450 us -> 430 us (0.956)
  waiting for transfers between devices: 312 us -> 296 us
    all_to_all x2, waiting for transfers between devices: 54 us -> 228 us  [on_device(): lax.all_to_all(spectra, ('grp', 'dev'), split_axis=0, concat_axis=0, tile...]
    psum x1, waiting for transfers between devices: 186 us -> 67.4 us  [on_device(): summed = lax.psum(kept, 'dev')]
    all_gather x1, waiting for transfers between devices: 71.6 us -> 0.02 us  [on_device(): weights = lax.all_gather(summed, 'grp', axis=1, tiled=True)]
  transfers between devices with their start and end apart: 4 -> 4, of which waited for: 3 -> 3; matrix products, arithmetic and copies ran while one was open for 4% -> 1% of each run, Pallas kernels for 10% -> 19%
where the time goes in v2:
time: 430 us
  waiting for transfers between devices  296 us (69%)
  Pallas kernels  92.5 us (22%)
  local copies, waits for them, and re-layouts  16.2 us (4%)
  between operations  13.5 us (3%)
  starting transfers between devices  8.29 us (2%)
    all_to_all x2, waiting for transfers between devices, on_device(): lax.all_to_all(spectra, ('grp', 'dev'), split_axis=0, concat_axis=0, tile...  228 us
    pallas_call x2, Pallas kernels, channelize(): pl.pallas_call(functools.partial(channelize_kernel, step, ants), grid=(an...  74.6 us
    psum x1, waiting for transfers between devices, on_device(): summed = lax.psum(kept, 'dev')  67.4 us
    pallas_call x2, Pallas kernels, detect(): pl.pallas_call(functools.partial(detect_kernel, sources, ants), grid=(2,)...  17.9 us
  transfers between devices with their start and end apart: 4, of which 3 were waited for; matrix products, arithmetic and copies ran while one was open for 1% of the time, Pallas kernels for 19%

profile of v2, /device:TPU:0, one launch (start us, length us, event | category | flops | bytes accessed | tf_op | source)
XLA Modules:
  0.0 429.9 jit_solution(9524328533828325889)
XLA Ops:
  6.5 0.0 all-reduce.2.cloned.1.call-start
  6.5 0.8 compare_and_fusion
  7.3 0.0 copy-start.1
  7.3 4.2 gather_fusion.1
  11.5 4.2 gather_fusion
  15.7 0.0 copy-done.1
  15.7 0.2 select_convert_fusion.1
  16.0 0.1 pad_maximum_fusion
  16.1 1.5 broadcast_select_fusion
  17.6 0.0 all-reduce.2.cloned.1.call-update
  17.6 37.3 %channelize.3 = bf16[32,16,16,384]{3,2,1,0:T(8,128)(2,1)} custom-call(bf16[64,110592]{1,0:T(8,128)(2,1)} %vr_ref.3, bf16[64,110592]{1,0:T(8,128)(2,1)} %vi_ref.3, f32[16,4096]{1,0:T(8,128)} %taps_ref.1, bf16[32,256,256]{2,1,0:T(8,128)(2,1)} %constant.30.clone.wh_ref, bf16[32,256,256]{2,1,0:T(8,128)(2,1)} %constant.31.clone.wl_ref), custom_call_target="tpu_custom_call" | custom-call | flops 20000000000 | bytes 50000000 | tf_op jit(solution)/shard_map/channelize/pallas_call | solution.py:141
  54.9 67.4 %all-reduce.2.cloned.1.call-done = bf16[2,512,1024]{2,1,0:T(8,128)(2,1)} async-done(((bf16[2,512,1024]{2,1,0:T(8,128)(2,1)}), bf16[2,512,1024]{2,1,0:T(8,128)(2,1)}) %all-reduce.2.cloned.1.call-update) | async-done | bytes 2097168 | tf_op jit(solution)/shard_map/psum | solution.py:236
  122.3 4.4 %all-to-all-start.1 = ((bf16[32,256,384]{2,1,0:T(8,128)(2,1)}), bf16[32,256,384]{2,1,0:T(8,128)(2,1)}, u32[]{:S(2)}, u32[]{:S(2)}) async-start(bf16[32,256,384]{2,1,0:T(8,128)(2,1)} %bitcast.13), calls=%async_computation.1 | async-start | bytes 12582912 | tf_op jit(solution)/shard_map/all_to_all | solution.py:249
  126.8 0.0 all-gather.2.cloned.1.call-start
  126.8 0.7 all-gather.2.cloned.1.call-update
  127.5 37.3 %channelize.2 = bf16[32,16,16,384]{3,2,1,0:T(8,128)(2,1)} custom-call(bf16[64,110592]{1,0:T(8,128)(2,1)} %vr_ref.3, bf16[64,110592]{1,0:T(8,128)(2,1)} %vi_ref.3, f32[16,4096]{1,0:T(8,128)} %taps_ref.1, bf16[32,256,256]{2,1,0:T(8,128)(2,1)} %constant.30.clone.wh_ref, bf16[32,256,256]{2,1,0:T(8,128)(2,1)} %constant.31.clone.wl_ref), custom_call_target="tpu_custom_call" | custom-call | flops 20000000000 | bytes 50000000 | tf_op jit(solution)/shard_map/channelize/pallas_call | solution.py:141
  164.9 102.2 %all-to-all-done.1.x_ref = bf16[32,256,384]{2,1,0:T(8,128)(2,1)} async-done(((bf16[32,256,384]{2,1,0:T(8,128)(2,1)}), bf16[32,256,384]{2,1,0:T(8,128)(2,1)}, u32[]{:S(2)}, u32[]{:S(2)}) %all-to-all-start.1) | async-done | bytes 6291488 | tf_op jit(solution)/shard_map/all_to_all | solution.py:249
  267.0 3.8 all-to-all-start
  270.9 0.0 all-gather.2.cloned.1.call-done
  270.9 5.3 %slice_bitcast_fusion.1 = (bf16[2048,1024]{1,0:T(8,128)(2,1)}, bf16[2048,1024]{1,0:T(8,128)(2,1)S(1)}) fusion(bf16[2,2048,1024]{2,1,0:T(8,128)(2,1)} %all-gather.2.cloned.1.call-done), kind=kLoop, calls=%fused_computation.3 | loop fusion | bytes 16777216 | tf_op jit(solution)/shard_map/squeeze | solution.py:254
  276.2 9.0 %detect.3 = f32[128,512]{1,0:T(8,128)S(1)} custom-call(bf16[32,256,384]{2,1,0:T(8,128)(2,1)} %all-to-all-done.1.x_ref, bf16[2048,1024]{1,0:T(8,128)(2,1)S(1)} %get-tuple-element.17.w_ref), custom_call_target="tpu_custom_call" | custom-call | flops 6499999744 | bytes 11000000 | tf_op jit(solution)/shard_map/detect/pallas_call | solution.py:191
  285.1 0.1 reshape.22
  285.2 0.1 copy.11
  285.3 125.5 %all-to-all-done.x_ref = bf16[32,256,384]{2,1,0:T(8,128)(2,1)} async-done(((bf16[32,256,384]{2,1,0:T(8,128)(2,1)}), bf16[32,256,384]{2,1,0:T(8,128)(2,1)}, u32[]{:S(2)}, u32[]{:S(2)}) %all-to-all-start) | async-done | bytes 6291488 | tf_op jit(solution)/shard_map/all_to_all | solution.py:249
  410.9 0.0 copy-start
  410.9 2.2 copy-done
  413.0 9.0 %detect.2 = f32[128,512]{1,0:T(8,128)S(1)} custom-call(bf16[32,256,384]{2,1,0:T(8,128)(2,1)} %all-to-all-done.x_ref, bf16[2048,1024]{1,0:T(8,128)(2,1)S(1)} %copy-done), custom_call_target="tpu_custom_call" | custom-call | flops 6499999744 | bytes 11000000 | tf_op jit(solution)/shard_map/detect/pallas_call | solution.py:191
  422.0 0.1 reshape.21
  422.1 0.1 copy.10
  422.2 0.8 pad_maximum_fusion.1
  (2 shorter events, 0.0 us)
Async XLA Ops:
  6.5 115.8 %all-reduce.2.cloned.1.call-start = ((), (), s32[]{:S(2)}) async-start(), calls=%async_computation.2 | async-start | bytes 4194304 | tf_op jit(solution)/shard_map/psum | solution.py:236
  7.3 8.4 %copy-start.1 = (s32[2]{0:T(128)S(1)}, s32[2]{0:T(128)}, u32[]{:S(2)}) copy-start(s32[2]{0:T(128)} %param.16) | copy-start | bytes 28
  122.3 144.7 %all-to-all-start.1 = ((bf16[32,256,384]{2,1,0:T(8,128)(2,1)}), bf16[32,256,384]{2,1,0:T(8,128)(2,1)}, u32[]{:S(2)}, u32[]{:S(2)}) async-start(bf16[32,256,384]{2,1,0:T(8,128)(2,1)} %bitcast.13), calls=%async_computation.1 | async-start | bytes 12582912 | tf_op jit(solution)/shard_map/all_to_all | solution.py:249
  126.8 144.1 %all-gather.2.cloned.1.call-start = ((), (), s32[]{:S(2)}) async-start(), calls=%async_computation.3 | async-start | bytes 10485760 | tf_op jit(solution)/shard_map/all_gather | solution.py:250
  267.0 143.8 %all-to-all-start = ((bf16[32,256,384]{2,1,0:T(8,128)(2,1)}), bf16[32,256,384]{2,1,0:T(8,128)(2,1)}, u32[]{:S(2)}, u32[]{:S(2)}) async-start(bf16[32,256,384]{2,1,0:T(8,128)(2,1)} %bitcast.12), calls=%async_computation | async-start | bytes 12582912 | tf_op jit(solution)/shard_map/all_to_all | solution.py:249
  410.9 2.2 copy-start
Sparse Core Ops, SparseCore 0:
  17.8 104.5 all-reduce.1
  129.2 112.4 all-gather.1
